TPU v7x, 512 devices: a whole 4x8x8 slice. The times are simulated.
512 devices in a mesh: req: 64 (over z, x, core), tp: 8 (over y).
Axes of the slice: x: 4, y: 8, z: 8, core: 2. Of those that a mesh axis runs over, the one named last changes fastest.
Arguments:
- normed_hidden_input: bfloat16 [1024, 2, 8192], P('req', None, 'tp'), may hold values from -6 to 6
- value_matrix: bfloat16 [8192, 1024], P(None, 'tp'), may hold values from -0.0625 to 0.0625
- adapter_down_weight: bfloat16 [8192, 32768], P('tp', 'req'), may hold values from -0.0625 to 0.0625
- adapter_up_weight: bfloat16 [32768, 1024], P('req', 'tp'), may hold values from -0.75 to 0.75
- request_adapter: int32 [1024], P('req'), may hold values from 0 to 511, as said below
- adapter_storage_row: int32 [512], replicated, may hold values from 0 to 511, as said below
- cache_valid_length: int32 [1024], P('req'), may hold values from 2 to 64
- queries: bfloat16 [1024, 2, 8192], P('req', None, 'tp'), may hold values from -9 to 9
- stored_key_cache: bfloat16 [1024, 64, 1024], P('req', None, 'tp'), may hold values from -4 to 4
- stored_value_cache: bfloat16 [1024, 64, 1024], P('req', None, 'tp'), may hold values from -6 to 6
- step_keys: bfloat16 [1024, 2, 1024], P('req', None, 'tp'), may hold values from -6 to 6
Outputs:
- step_values: bfloat16 [1024, 2, 1024], P('req', None, 'tp')
- attention: bfloat16 [1024, 2, 8192], P('req', None, 'tp')
Inputs may be any that keep to these rules, and one draw needn't show every extreme that they name: `request_adapter`: storage row p lies on home device p // 8. Of the 16 requests of one device, at most 2 use adapters stored on one home device; one home device gets exactly 2 from every device. `adapter_storage_row`: A permutation.
All inputs are finite; a program needn't handle non-finite values.
Results may differ from a plain program's by a relative error of at most 0.0053.
Values may be sent and summed in bfloat16 or wider, within the bound.
No kernel may reach another device: no remote copies, remote signals or barrier semaphores. Data moves between devices by JAX's collectives and lax.ppermute only.
A program may use at most 64 MiB of HBM per device.

v0:
```python
import math
import jax
import jax.numpy as jnp
from jax import lax
from jax.sharding import PartitionSpec as P

HEAD_WIDTH = 128
ADAPTER_RANK = 64
QUERY_PER_KEY = 8


def body(
    normed_hidden_input,
    value_matrix,
    adapter_down_weight,
    adapter_up_weight,
    request_adapter,
    adapter_storage_row,
    cache_valid_length,
    queries,
    stored_key_cache,
    stored_value_cache,
    step_keys,
):
    req_local, step_count, width_local = normed_hidden_input.shape
    value_local = value_matrix.shape[1]
    adapter_delta = adapter_up_weight.shape[0] // ADAPTER_RANK
    my_index = lax.axis_index("req")
    total_adapters = adapter_storage_row.shape[0]
    matches = request_adapter[:, None] == jnp.arange(total_adapters, dtype=jnp.int32)[None, :]
    storage = jnp.sum(jnp.where(matches, adapter_storage_row[None, :], 0), axis=1)
    columns_in = lax.all_gather(normed_hidden_input, "tp", axis=2, tiled=True)
    span = columns_in.shape[2]
    product = jnp.dot(
        columns_in.reshape(-1, span), value_matrix, preferred_element_type=jnp.float32
    )
    plain_values = product.reshape(
        jnp.zeros((req_local, step_count, value_local), jnp.float32).shape
    )
    every_row, every_storage = (
        lax.all_gather(normed_hidden_input, "req", axis=0, tiled=True),
        lax.all_gather(storage, "req", axis=0, tiled=True),
    )
    every_slot = jnp.where(
        every_storage // adapter_delta == my_index, every_storage % adapter_delta, -1
    )
    row_count = every_row.shape[0]
    projected = jnp.dot(
        every_row.reshape(row_count * step_count, width_local),
        adapter_down_weight,
        preferred_element_type=jnp.float32,
    )
    projected = projected.reshape(row_count, step_count, adapter_delta, ADAPTER_RANK)
    chosen = (every_slot[:, None] == jnp.arange(adapter_delta, dtype=jnp.int32)[None, :]).astype(
        jnp.float32
    )
    partial_value = jnp.einsum("nsar,na->nsr", projected, chosen)
    summed_all = lax.psum(partial_value, "tp").astype(jnp.bfloat16)
    row_count = summed_all.shape[0]
    chosen = (
        every_slot[:, None, None, None]
        == jnp.arange(adapter_delta, dtype=jnp.int32)[None, None, :, None]
    )
    spread = jnp.where(chosen, summed_all[:, :, None, :], jnp.zeros((), jnp.bfloat16))
    product = jnp.dot(
        spread.reshape(row_count * step_count, adapter_delta * ADAPTER_RANK),
        adapter_up_weight,
        preferred_element_type=jnp.float32,
    )
    low_rank = lax.psum_scatter(
        product.reshape(row_count, step_count, value_local), "req", scatter_dimension=0, tiled=True
    ).astype(jnp.bfloat16)
    low_rank = lax.optimization_barrier(low_rank)
    step_values = (plain_values + low_rank.astype(jnp.float32)).astype(jnp.bfloat16)
    kv_local = value_local // HEAD_WIDTH
    scale = 1.0 / math.sqrt(HEAD_WIDTH)
    query_head_view = queries.reshape(req_local, step_count, kv_local, QUERY_PER_KEY, HEAD_WIDTH)
    key_head_view = stored_key_cache.reshape(req_local, -1, kv_local, HEAD_WIDTH)
    value_view = stored_value_cache.reshape(req_local, -1, kv_local, HEAD_WIDTH)
    current_keys = step_keys.reshape(req_local, step_count, kv_local, HEAD_WIDTH)
    fresh_values = step_values.reshape(req_local, step_count, kv_local, HEAD_WIDTH)
    context = key_head_view.shape[1]
    cache_scores = (
        jnp.einsum(
            "rskgd,rckd->rskgc", query_head_view, key_head_view, preferred_element_type=jnp.float32
        )
        * scale
    )
    fresh_scores = (
        jnp.einsum(
            "rskgd,rtkd->rskgt", query_head_view, current_keys, preferred_element_type=jnp.float32
        )
        * scale
    )
    valid = jnp.arange(context, dtype=jnp.int32)[None, :] < cache_valid_length[:, None]
    causal = (
        jnp.arange(step_count, dtype=jnp.int32)[None, :]
        <= jnp.arange(step_count, dtype=jnp.int32)[:, None]
    )
    cache_scores = jnp.where(valid[:, None, None, None, :], cache_scores, -jnp.inf)
    fresh_scores = jnp.where(causal[None, :, None, None, :], fresh_scores, -jnp.inf)
    peak = jnp.maximum(jnp.max(cache_scores, axis=-1), jnp.max(fresh_scores, axis=-1))[..., None]
    cache_expo = jnp.exp(cache_scores - peak)
    fresh_expo = jnp.exp(fresh_scores - peak)
    denominator = jnp.sum(cache_expo, axis=-1, keepdims=True) + jnp.sum(
        fresh_expo, axis=-1, keepdims=True
    )
    cache_weights = (cache_expo / denominator).astype(jnp.bfloat16)
    fresh_weights = (fresh_expo / denominator).astype(jnp.bfloat16)
    attended = jnp.einsum(
        "rskgc,rckd->rskgd", cache_weights, value_view, preferred_element_type=jnp.float32
    )
    attended = attended + jnp.einsum(
        "rskgt,rtkd->rskgd", fresh_weights, fresh_values, preferred_element_type=jnp.float32
    )
    attention = attended.astype(jnp.bfloat16).reshape(
        req_local, step_count, kv_local * QUERY_PER_KEY * HEAD_WIDTH
    )
    return (step_values, attention)


def solution(mesh):
    placed = (
        P("req", None, "tp"),
        P(None, "tp"),
        P("tp", "req"),
        P("req", "tp"),
        P("req"),
        P(),
        P("req"),
        P("req", None, "tp"),
        P("req", None, "tp"),
        P("req", None, "tp"),
        P("req", None, "tp"),
    )
    return jax.shard_map(
        body,
        mesh=mesh,
        in_specs=placed,
        out_specs=(P("req", None, "tp"), P("req", None, "tp")),
        check_vma=False,
    )
```

profile of v0, /device:TPU:8, one launch (start us, length us, event | category | flops | bytes accessed | tf_op | source)
XLA Modules:
  0.0 298.1 jit_solution(1287845142571132430)
XLA Ops:
  7.2 0.0 copy-start
  7.2 0.0 copy-start.7
  7.2 0.0 copy-start.5
  7.2 0.0 all-gather.2.cloned.1.call-start
  7.2 0.7 all-gather.2.cloned.1.call-update
  7.9 0.0 reduce-scatter.2.cloned.1.call-start
  8.0 1.5 copy.28
  9.5 1.3 dynamic-slice
  11.4 0.0 copy-done.7
  11.4 0.0 copy-done.5
  11.4 0.2 select_reduce_fusion
  11.6 0.2 dynamic-update-slice
  11.9 26.9 %all-reduce = s32[1024]{0:T(1024)S(1)} all-reduce(s32[1024]{0:T(1024)S(1)} %dynamic-update-slice), channel_id=1, replica_groups=mesh['req'=64,'tp'=8] {'req'}, use_global_device_ids=true, to_apply=%add | all-reduce | flops 1024 | bytes 8192
  38.8 62.3 %all-gather.2.cloned.1.call-done = bf16[1024,2,1024]{2,1,0:T(2,128)(2,1)} async-done(((bf16[16,2,1024]{2,1,0:T(2,128)(2,1)}), bf16[1024,2,1024]{2,1,0:T(2,128)(2,1)}) %all-gather.2.cloned.1.call-update) | async-done | bytes 4194320 | tf_op jit(solution)/shard_map/all_gather | solution.py:41
  101.1 5.5 %multiply_reduce_fusion = f32[1024,2,64]{0,2,1:T(8,128)} fusion(bf16[8,64,1024,1]{2,1,0,3:T(8,128)(2,1)S(1)} %bitcast.84, bf16[1024,2,1024,1]{2,1,0,3:T(2,128)(2,1)} %bitcast.86, f32[1024,8]{0,1:T(8,128)S(1)} %get-tuple-element.10), kind=kOutput, calls=%fused_computation.2 | convolution fusion | flops 2149449728 | bytes 5799936 | tf_op jit(solution)/shard_map/dot_general | solution.py:48
  106.6 0.0 copy-start.3
  106.6 35.4 %all-reduce.2 = bf16[1024,2,64]{0,2,1:T(8,128)(2,1)S(1)} all-reduce(f32[1024,2,64]{0,2,1:T(8,128)} %multiply_reduce_fusion), channel_id=1, replica_groups=mesh['req'=64,'tp'=8] {'tp'}, use_global_device_ids=true, to_apply=%region_1.2 | all-reduce | flops 131072 | bytes 786432 | tf_op jit(solution)/shard_map/psum | solution.py:58
  142.0 0.1 broadcast_in_dim.83
  142.2 0.3 bitcast_select_fusion
  142.5 0.0 copy-done.3
  142.5 0.0 copy-start.2
  142.5 0.0 copy-start.4
  142.5 0.0 copy-start.6
  142.5 0.0 copy-start.9
  142.6 0.0 copy-start.1
  142.6 1.7 fusion.22
  144.3 0.0 reduce-scatter.2.cloned.1.call-update
  144.3 0.0 copy-done.2
  144.4 0.0 copy-done.4
  144.4 0.0 copy-done.6
  144.5 0.1 iota_compare_fusion.2
  144.5 0.0 copy-done.9
  144.5 0.4 fusion.39
  145.0 0.0 copy-done.1
  145.0 0.3 fusion.38
  145.3 0.0 copy-start.8
  145.3 0.1 fusion.27
  145.4 0.2 fusion.24
  145.6 25.3 %all_gather.9 = bf16[16,2,8192]{2,0,1:T(8,128)(2,1)S(1)} all-gather(bf16[16,2,1024]{2,0,1:T(8,128)(2,1)S(1)} %copy.27), channel_id=1, replica_groups=mesh['req'=64,'tp'=8] {'tp'}, dimensions={2}, use_global_device_ids=true | all-gather | bytes 589824 | tf_op jit(solution)/shard_map/all_gather | solution.py:32
  171.0 117.4 %reduce-scatter.2.cloned.1.call-done = f32[16,2,128]{2,0,1:T(8,128)} async-done(((f32[1024,2,128]{2,0,1:T(8,128)}), f32[16,2,128]{2,0,1:T(8,128)}) %reduce-scatter.2.cloned.1.call-update) | async-done | bytes 16400 | tf_op jit(solution)/shard_map/reduce_scatter | solution.py:70
  288.4 0.7 convert_element_type.29
  289.1 0.0 copy-done
  289.1 0.4 fusion.16
  289.5 0.6 copy.32
  290.1 0.2 fusion.28
  290.4 0.0 copy-done.8
  290.4 0.3 fusion.11
  290.6 0.7 reshape.157
  (8 shorter events, 0.1 us)
Async XLA Ops:
  7.2 281.9 %copy-start = (bf16[8192,128]{1,0:T(8,128)(2,1)S(1)}, bf16[8192,128]{1,0:T(8,128)(2,1)}, u32[]{:S(2)}) copy-start(bf16[8192,128]{1,0:T(8,128)(2,1)} %param.12) | copy-start | bytes 6291460
  7.2 4.2 %copy-start.7 = (s32[16]{0:T(128)S(1)}, s32[16]{0:T(128)}, u32[]{:S(2)}) copy-start(s32[16]{0:T(128)} %param.15) | copy-start | bytes 196
  7.2 4.2 %copy-start.5 = (s32[512]{0:T(512)S(1)}, s32[512]{0:T(512)}, u32[]{:S(2)}) copy-start(s32[512]{0:T(512)} %param.16) | copy-start | bytes 6148
  7.2 93.9 %all-gather.2.cloned.1.call-start = ((), (), s32[]{:S(2)}) async-start(), calls=%async_computation.1 | async-start | bytes 4259840 | tf_op jit(solution)/shard_map/all_gather | solution.py:41
  7.9 280.4 %reduce-scatter.2.cloned.1.call-start = ((), (), s32[]{:S(2)}) async-start(), calls=%async_computation.2 | async-start | bytes 1064960 | tf_op jit(solution)/shard_map/reduce_scatter | solution.py:70
  106.6 35.9 %copy-start.3 = (bf16[512,128]{1,0:T(8,128)(2,1)S(1)}, bf16[512,128]{1,0:T(8,128)(2,1)}, u32[]{:S(2)}) copy-start(bf16[512,128]{1,0:T(8,128)(2,1)} %param.14) | copy-start | bytes 393220
  142.5 1.8 copy-start.2
  142.5 1.9 copy-start.4
  142.5 1.9 copy-start.6
  142.5 2.0 copy-start.9
  142.6 2.4 copy-start.1
  145.3 145.1 %copy-start.8 = (bf16[16,64,128]{2,1,0:T(8,128)(2,1)S(1)}, bf16[16,64,128]{2,1,0:T(8,128)(2,1)}, u32[]{:S(2)}) copy-start(bf16[16,64,128]{2,1,0:T(8,128)(2,1)} %param.20) | copy-start | bytes 786436
Sparse Core Ops, SparseCore 0:
  11.4 89.6 all-gather.1
  144.5 143.8 reduce-scatter.1
where the time goes:
time: 298 us
  waiting for transfers between devices  180 us (60%)
  blocking collectives  87.7 us (29%)
  between operations  14.9 us (5%)
  matrix products  8.95 us (3%)
  local copies, waits for them, and re-layouts  4.54 us (2%)
    reduce_scatter x1, waiting for transfers between devices, body(): lax.psum_scatter(product.reshape(row_count, step_count, value_local), 're...  117 us
    all_gather x1, waiting for transfers between devices, body(): lax.all_gather(normed_hidden_input, 'req', axis=0, tiled=True)  62.3 us
    psum x1, blocking collectives, body(): summed_all = lax.psum(partial_value, 'tp').astype(jnp.bfloat16)  35.4 us
    unnamed x1, blocking collectives  26.9 us
    all_gather x1, blocking collectives, body(): columns_in = lax.all_gather(normed_hidden_input, 'tp', axis=2, tiled=True)  25.3 us
  transfers between devices with their start and end apart: 2, of which 2 were waited for; matrix products, arithmetic and copies ran while one was open for 1% of the time, Pallas kernels for 0%

commit v1 on v0

--- a/solution.py
+++ b/solution.py
@@ -3,10 +3,16 @@
 import jax.numpy as jnp
 from jax import lax
 from jax.sharding import PartitionSpec as P
+from jax.lax import all_gather
 
 HEAD_WIDTH = 128
 ADAPTER_RANK = 64
 QUERY_PER_KEY = 8
+
+
+def _put_links(m):
+    mat_out = all_gather(m, axis_name="tp").sum(axis=0)
+    return mat_out
 
 
 def body(
@@ -55,7 +61,7 @@
         jnp.float32
     )
     partial_value = jnp.einsum("nsar,na->nsr", projected, chosen)
-    summed_all = lax.psum(partial_value, "tp").astype(jnp.bfloat16)
+    summed_all = _put_links(partial_value).astype(jnp.bfloat16)
     row_count = summed_all.shape[0]
     chosen = (
         every_slot[:, None, None, None]

time: 298 us -> 332 us (1.11)
  waiting for transfers between devices: 180 us -> 237 us
  blocking collectives: 87.7 us -> 53.5 us
  local copies, waits for them, and re-layouts: 4.54 us -> 12.7 us
    all_gather x0 -> x1, waiting for transfers between devices: none -> 52.7 us  [_put_links(): mat_out = all_gather(m, axis_name='tp').sum(axis=0)]
    psum x1 -> x0, blocking collectives: 35.4 us -> none  [body(): summed_all = lax.psum(partial_value, 'tp').astype(jnp.bfloat16)]
    unnamed x26 -> x27, local copies, waits for them, and re-layouts: 3.69 us -> 11.8 us
    reduce_scatter x1, waiting for transfers between devices: 117 us -> 121 us  [body(): lax.psum_scatter(product.reshape(row_count, step_count, value_local), 're...]
  transfers between devices with their start and end apart: 2 -> 3, of which waited for: 2 -> 3; matrix products, arithmetic and copies ran while one was open for 1% -> 1% of each run, Pallas kernels for 0% -> 0%
where the time goes in v1:
time: 332 us; the launch traced here: 331 us
  waiting for transfers between devices  237 us (71%)
  blocking collectives  53.5 us (16%)
  between operations  14.6 us (4%)
  local copies, waits for them, and re-layouts  12.7 us (4%)
  matrix products  8.95 us (3%)
  other arithmetic  4.84 us (1%)
    reduce_scatter x1, waiting for transfers between devices, body(): lax.psum_scatter(product.reshape(row_count, step_count, value_local), 're...  121 us
    all_gather x1, waiting for transfers between devices, body(): lax.all_gather(normed_hidden_input, 'req', axis=0, tiled=True)  62.3 us
    all_gather x1, waiting for transfers between devices, _put_links(): mat_out = all_gather(m, axis_name='tp').sum(axis=0)  52.7 us
    unnamed x1, blocking collectives  26.9 us
    all_gather x1, blocking collectives, body(): columns_in = lax.all_gather(normed_hidden_input, 'tp', axis=2, tiled=True)  26.5 us
    unnamed x27, local copies, waits for them, and re-layouts  11.8 us
  transfers between devices with their start and end apart: 3, of which 3 were waited for; matrix products, arithmetic and copies ran while one was open for 1% of the time, Pallas kernels for 0%

profile of v1, /device:TPU:8, one launch (start us, length us, event | category | flops | bytes accessed | tf_op | source)
XLA Modules:
  0.0 331.4 jit_solution(10626191122772089524)
XLA Ops:
  7.2 0.0 copy-start
  7.2 0.0 copy-start.7
  7.2 0.0 copy-start.5
  7.2 0.0 all-gather.4.cloned.1.call-start
  7.2 0.7 all-gather.4.cloned.1.call-update
  7.9 0.0 all-gather.6.cloned.1.call-start
  8.0 1.5 copy.28
  9.5 1.3 dynamic-slice
  11.4 0.0 copy-done.7
  11.4 0.0 copy-done.5
  11.4 0.2 select_reduce_fusion
  11.6 0.2 dynamic-update-slice
  11.9 26.9 %all-reduce = s32[1024]{0:T(1024)S(1)} all-reduce(s32[1024]{0:T(1024)S(1)} %dynamic-update-slice), channel_id=1, replica_groups=mesh['req'=64,'tp'=8] {'req'}, use_global_device_ids=true, to_apply=%add | all-reduce | flops 1024 | bytes 8192
  38.8 62.3 %all-gather.4.cloned.1.call-done = bf16[1024,2,1024]{2,1,0:T(2,128)(2,1)} async-done(((bf16[16,2,1024]{2,1,0:T(2,128)(2,1)}), bf16[1024,2,1024]{2,1,0:T(2,128)(2,1)}) %all-gather.4.cloned.1.call-update) | async-done | bytes 4194320 | tf_op jit(solution)/shard_map/all_gather | solution.py:47
  101.1 5.5 %multiply_reduce_fusion = f32[1024,2,64]{0,2,1:T(8,128)} fusion(bf16[8,64,1024,1]{2,1,0,3:T(8,128)(2,1)S(1)} %bitcast.92, bf16[1024,2,1024,1]{2,1,0,3:T(2,128)(2,1)} %bitcast.94, f32[1024,8]{0,1:T(8,128)S(1)} %get-tuple-element.10), kind=kOutput, calls=%fused_computation.2 | convolution fusion | flops 2149449728 | bytes 5799936 | tf_op jit(solution)/shard_map/dot_general | solution.py:54
  106.6 0.0 all-gather.6.cloned.1.call-update
  106.6 0.0 reduce-scatter.2.cloned.1.call-start
  106.7 52.7 %all-gather.6.cloned.1.call-done = f32[8192,2,64]{0,2,1:T(8,128)} async-done(((f32[1024,2,64]{0,2,1:T(8,128)}), f32[8192,2,64]{0,2,1:T(8,128)}) %all-gather.6.cloned.1.call-update) | async-done | bytes 4194320 | tf_op jit(solution)/shard_map/all_gather | solution.py:14
  159.4 7.7 %copy.49 = f32[16,8,8,1024]{3,2,1,0:T(8,128)} copy(f32[16,8,8,1024]{3,1,2,0:T(8,128)} %bitcast.90) | data formatting | bytes 8388608
  167.1 3.2 reduce_sum.37
  170.3 0.0 copy-start.3
  170.4 0.1 broadcast_in_dim.83
  170.5 0.3 bitcast_select_fusion
  170.8 0.4 copy-done.3
  171.3 0.0 copy-start.2
  171.3 0.0 copy-start.4
  171.3 0.0 copy-start.6
  171.3 0.0 copy-start.9
  171.3 0.0 copy-start.1
  171.3 1.7 fusion.22
  173.0 0.0 reduce-scatter.2.cloned.1.call-update
  173.0 0.0 copy-done.2
  173.1 0.0 copy-done.4
  173.1 0.0 copy-done.6
  173.2 0.1 iota_compare_fusion.2
  173.2 0.0 copy-done.9
  173.2 0.4 fusion.39
  173.7 0.0 copy-done.1
  173.7 0.3 fusion.38
  174.0 0.0 copy-start.8
  174.0 0.1 fusion.27
  174.1 0.2 fusion.24
  174.3 26.5 %all_gather.15 = bf16[16,2,8192]{2,0,1:T(8,128)(2,1)S(1)} all-gather(bf16[16,2,1024]{2,0,1:T(8,128)(2,1)S(1)} %copy.27), channel_id=1, replica_groups=mesh['req'=64,'tp'=8] {'tp'}, dimensions={2}, use_global_device_ids=true | all-gather | bytes 589824 | tf_op jit(solution)/shard_map/all_gather | solution.py:38
  200.9 121.1 %reduce-scatter.2.cloned.1.call-done = f32[16,2,128]{2,0,1:T(8,128)} async-done(((f32[1024,2,128]{2,0,1:T(8,128)}), f32[16,2,128]{2,0,1:T(8,128)}) %reduce-scatter.2.cloned.1.call-update) | async-done | bytes 16400 | tf_op jit(solution)/shard_map/reduce_scatter | solution.py:76
  321.9 0.7 convert_element_type.33
  322.6 0.0 copy-done
  322.7 0.4 fusion.16
  323.1 0.6 copy.32
  323.7 0.2 fusion.28
  323.9 0.0 copy-done.8
  323.9 0.3 fusion.11
  324.2 0.7 reshape.159
  (8 shorter events, 0.1 us)
Async XLA Ops:
  7.2 315.5 %copy-start = (bf16[8192,128]{1,0:T(8,128)(2,1)S(1)}, bf16[8192,128]{1,0:T(8,128)(2,1)}, u32[]{:S(2)}) copy-start(bf16[8192,128]{1,0:T(8,128)(2,1)} %param.12) | copy-start | bytes 6291460
  7.2 4.2 %copy-start.7 = (s32[16]{0:T(128)S(1)}, s32[16]{0:T(128)}, u32[]{:S(2)}) copy-start(s32[16]{0:T(128)} %param.15) | copy-start | bytes 196
  7.2 4.2 %copy-start.5 = (s32[512]{0:T(512)S(1)}, s32[512]{0:T(512)}, u32[]{:S(2)}) copy-start(s32[512]{0:T(512)} %param.16) | copy-start | bytes 6148
  7.2 93.9 %all-gather.4.cloned.1.call-start = ((), (), s32[]{:S(2)}) async-start(), calls=%async_computation.1 | async-start | bytes 4259840 | tf_op jit(solution)/shard_map/all_gather | solution.py:47
  7.9 151.5 %all-gather.6.cloned.1.call-start = ((), (), s32[]{:S(2)}) async-start(), calls=%async_computation.3 | async-start | bytes 4718592 | tf_op jit(solution)/shard_map/all_gather | solution.py:14
  106.6 215.3 %reduce-scatter.2.cloned.1.call-start = ((), (), s32[]{:S(2)}) async-start(), calls=%async_computation.2 | async-start | bytes 1064960 | tf_op jit(solution)/shard_map/reduce_scatter | solution.py:76
  170.3 0.9 copy-start.3
  171.3 1.8 copy-start.2
  171.3 1.8 copy-start.4
  171.3 1.9 copy-start.6
  171.3 2.0 copy-start.9
  171.3 2.4 copy-start.1
  174.0 149.9 %copy-start.8 = (bf16[16,64,128]{2,1,0:T(8,128)(2,1)S(1)}, bf16[16,64,128]{2,1,0:T(8,128)(2,1)}, u32[]{:S(2)}) copy-start(bf16[16,64,128]{2,1,0:T(8,128)(2,1)} %param.20) | copy-start | bytes 786436
Sparse Core Ops, SparseCore 0:
  11.4 89.6 all-gather.3
  106.8 52.5 all-gather.5
  173.2 148.7 reduce-scatter.1
